TPU v7x, 32 devices: a whole 2x2x4 slice. The times are simulated.
32 devices in a mesh: expert: 4 (over y, x), dp: 8 (over z, core).
Axes of the slice: x: 2, y: 2, z: 4, core: 2. Of those that a mesh axis runs over, the one named last changes fastest.
Arguments:
- tokens: bfloat16 [4096, 2048], P(('expert', 'dp')), may hold values from -6 to 6
- cotangent: bfloat16 [4096, 2048], P(('expert', 'dp')), may hold values from -3 to 3
- w_in: bfloat16 [4, 2048, 768], P('expert', 'dp'), may hold values from -0.125 to 0.125
- w_out: bfloat16 [4, 2048, 384], P('expert', 'dp'), may hold values from -0.3125 to 0.3125
- block_rows: int32 [32, 4, 64], P(('expert', 'dp')), may hold values from -1 to 127, as said below
- block_gates: float32 [32, 4, 64], P(('expert', 'dp')), may hold values from 0.1 to 1
- block_count: int32 [32, 2], P(('expert', 'dp')), may hold values from 1 to 2, as said below
Outputs:
- mixed: bfloat16 [4096, 2048], P(('expert', 'dp'))
- token_grad: bfloat16 [4096, 2048], P(('expert', 'dp'))
- gate_grad: float32 [32, 4, 64], P(('expert', 'dp'))
- grad_in: bfloat16 [4, 2048, 768], P('expert', 'dp')
- grad_out: bfloat16 [4, 2048, 384], P('expert', 'dp')
Inputs may be any that keep to these rules, and one draw needn't show every extreme that they name: `block_rows`: for each shard and stop, the first block_count blocks list the tokens routed to that stop's expert in increasing order, followed by -1 entries to the end of the last used block; blocks beyond block_count hold arbitrary tokens of the shard. In every shard one stop receives all 128 tokens; each other stop receives a share of them that differs from shard to shard. `block_count`: the number of used blocks of each stop: the stop's routed tokens divided by 64, rounded up.
All inputs are finite; a program needn't handle non-finite values.
Results may differ from a plain program's by a relative error of at most 0.019.
Values may be sent and summed in bfloat16 or wider, within the bound.
A program may use at most 64 MiB of HBM per device.

v0:
```python
import jax
import jax.numpy as jnp
from jax import lax
from jax.sharding import PartitionSpec as P


def shifted(block, axis, distance):
    devices = range(lax.axis_size(axis))
    route = [((i - distance) % len(devices), i) for i in devices]
    return lax.ppermute(block, axis, route)


def silu_pair(preact):
    sigmoid_val = jax.nn.sigmoid(preact)
    return (preact * sigmoid_val, sigmoid_val * (1.0 + preact * (1.0 - sigmoid_val)))


def contract_rows(left_mat, right_mat):
    return lax.dot_general(
        left_mat, right_mat, (((0,), (0,)), ((), ())), preferred_element_type=jnp.float32
    )


def contract_cols(left_mat, right_mat):
    return lax.dot_general(
        left_mat, right_mat, (((1,), (1,)), ((), ())), preferred_element_type=jnp.float32
    )


def expert_pass(inputs, gated_cot, slab_in, slab_out):
    hidden_width = slab_out.shape[1]
    preact = jnp.dot(inputs, slab_in, preferred_element_type=jnp.float32)
    gate_pre = preact[:, :hidden_width]
    up_pre = preact[:, hidden_width:]
    activated, derivative = silu_pair(gate_pre)
    hidden = (activated * up_pre).astype(jnp.bfloat16)
    output = contract_cols(hidden, slab_out)
    act_grad = jnp.dot(gated_cot, slab_out, preferred_element_type=jnp.float32)
    hid_grad = jnp.concatenate(
        [act_grad * up_pre * derivative, act_grad * activated], axis=1
    ).astype(jnp.bfloat16)
    input_grad = contract_cols(hid_grad, slab_in)
    return (output, input_grad, hidden, hid_grad)


def term_maker(inputs, gated_cot, hidden, hid_grad):

    def partial_term(offset, extent):
        return jnp.concatenate(
            [contract_rows(inputs, hid_grad), contract_rows(gated_cot, hidden)], axis=1
        )

    return partial_term


def body(tokens, cotangent, w_in, w_out, block_rows, block_gates, block_count):
    stop_total = block_count.shape[1]
    block_size = block_rows.shape[2]
    slot_span = block_rows.shape[1] // stop_total * block_size
    row_table = block_rows.reshape(stop_total, slot_span)
    gate_table = block_gates.reshape(stop_total, slot_span)
    counts = block_count[0]
    shard_rows = w_in.shape[1]
    hidden_width = w_out.shape[2]
    positions = jnp.arange(slot_span, dtype=jnp.int32)
    mixed_sum = jnp.zeros(tokens.shape, jnp.float32)
    token_sum = jnp.zeros(tokens.shape, jnp.float32)
    gate_list = []
    slab_in, slab_out = (
        lax.all_gather(w_in[0], "dp", axis=0, tiled=True),
        lax.all_gather(w_out[0], "dp", axis=0, tiled=True),
    )
    kept = []
    for station in range(stop_total):
        entries = row_table[station]
        live_mask = ((positions // block_size < counts[station]) & (entries >= 0)).astype(
            jnp.float32
        )
        token_ids = jnp.where(entries >= 0, entries, 0)
        weight = gate_table[station] * live_mask
        inputs = tokens[token_ids]
        cot_rows = cotangent[token_ids]
        gated_cot = (weight[:, None] * cot_rows.astype(jnp.float32)).astype(jnp.bfloat16)
        live_mask, token_ids, weight, inputs, cot_rows, gated_cot = (
            live_mask,
            token_ids,
            weight,
            inputs,
            cot_rows,
            gated_cot,
        )
        if station == 0:
            output, input_grad, hidden, hid_grad = expert_pass(inputs, gated_cot, slab_in, slab_out)
            kept.append((inputs, gated_cot, hidden, hid_grad))
        else:
            far_inputs, far_cot = shifted((inputs, gated_cot), "expert", -station)
            far_output, far_grad, hidden, hid_grad = expert_pass(
                far_inputs, far_cot, slab_in, slab_out
            )
            kept.append((far_inputs, far_cot, hidden, hid_grad))
            output, input_grad = (
                shifted(far_output.astype(jnp.bfloat16), "expert", station).astype(
                    far_output.dtype
                ),
                shifted(far_grad.astype(jnp.bfloat16), "expert", station).astype(far_grad.dtype),
            )
        mixed_sum = mixed_sum.at[token_ids].add(weight[:, None] * output)
        token_sum = token_sum.at[token_ids].add(input_grad)
        gate_list.append(live_mask * jnp.sum(output * cot_rows.astype(jnp.float32), axis=1))
    offset = jnp.int32(0)
    total_term = jnp.zeros((lax.axis_size("dp") * shard_rows, 3 * hidden_width), jnp.float32)
    for stored in kept:
        piece = term_maker(*stored)(offset, lax.axis_size("dp") * shard_rows).astype(jnp.bfloat16)
        piece = lax.optimization_barrier(piece)
        total_term = total_term + piece.astype(jnp.float32)
    running = lax.psum_scatter(
        total_term.astype(jnp.bfloat16), "dp", scatter_dimension=0, tiled=True
    ).astype(jnp.float32)
    gate_grad = jnp.stack(gate_list).reshape(1, stop_total * slot_span // block_size, block_size)
    grad_in = running[:, : 2 * hidden_width].astype(jnp.bfloat16)[None]
    grad_out = running[:, 2 * hidden_width :].astype(jnp.bfloat16)[None]
    return (
        mixed_sum.astype(jnp.bfloat16),
        token_sum.astype(jnp.bfloat16),
        gate_grad,
        grad_in,
        grad_out,
    )


def solution(mesh):
    in_specs = (
        P(("expert", "dp"), None),
        P(("expert", "dp"), None),
        P("expert", "dp", None),
        P("expert", "dp", None),
        P(("expert", "dp"), None, None),
        P(("expert", "dp"), None, None),
        P(("expert", "dp"), None),
    )
    out_specs = (
        P(("expert", "dp"), None),
        P(("expert", "dp"), None),
        P(("expert", "dp"), None, None),
        P("expert", "dp", None),
        P("expert", "dp", None),
    )
    return jax.shard_map(body, mesh=mesh, in_specs=in_specs, out_specs=out_specs, check_vma=False)
```

profile of v0, /device:TPU:0, one launch (start us, length us, event | category | flops | bytes accessed | tf_op | source)
XLA Modules:
  0.0 179.7 jit_solution(4563407295856576373)
XLA Ops:
  9.6 0.9 gather_fusion.1
  10.5 3.9 %collective-permute-start = (bf16[128,2048]{1,0:T(8,128)(2,1)S(1)}, bf16[128,2048]{1,0:T(8,128)(2,1)S(1)}, u32[]{:S(2)}, u32[]{:S(2)}) collective-permute-start(bf16[128,2048]{1,0:T(8,128)(2,1)S(1)} %gather_fusion.1), channel_id=1, source_target_pairs={{8,0},{16,8},{24,16},{0,24},{9,1},{17,9},{25,17},{1,25},{10,2},{18... | collective-permute-start | bytes 1572872 | tf_op jit(solution)/shard_map/ppermute | solution.py:10
  14.6 0.9 gather_fusion
  15.5 0.9 gather_fusion.2
  16.5 1.7 gather_fusion.3
  20.9 4.7 %collective-permute-done = bf16[128,2048]{1,0:T(8,128)(2,1)S(1)} collective-permute-done((bf16[128,2048]{1,0:T(8,128)(2,1)S(1)}, bf16[128,2048]{1,0:T(8,128)(2,1)S(1)}, u32[]{:S(2)}, u32[]{:S(2)}) %collective-permute-start) | collective-permute-done | bytes 524320 | tf_op jit(solution)/shard_map/ppermute | solution.py:10
  25.7 25.0 %all-gather.5.cloned.1.call-done = bf16[1,2048,768]{2,1,0:T(8,128)(2,1)} async-done(((bf16[1,256,768]{2,1,0:T(8,128)(2,1)}), bf16[1,2048,768]{2,1,0:T(8,128)(2,1)}) %all-gather.5.cloned.1.call-update) | async-done | bytes 3145744 | tf_op jit(solution)/shard_map/all_gather | solution.py:70
  50.7 2.5 %fusion.4 = f32[128,768]{1,0:T(8,128)S(1)} fusion(bf16[128,2048]{1,0:T(8,128)(2,1)S(1)} %collective-permute-done, bf16[1,2048,768]{2,1,0:T(8,128)(2,1)} %all-gather.5.cloned.1.call-done), kind=kOutput, calls=%fused_computation.17 | convolution fusion | flops 402653184 | bytes 4063232 | tf_op jit(solution)/shard_map/dot_general | solution.py:32
  53.9 22.4 %all-gather.7.cloned.1.call-done = bf16[1,2048,384]{2,1,0:T(8,128)(2,1)} async-done(((bf16[1,256,384]{2,1,0:T(8,128)(2,1)}), bf16[1,2048,384]{2,1,0:T(8,128)(2,1)}) %all-gather.7.cloned.1.call-update) | async-done | bytes 1572880 | tf_op jit(solution)/shard_map/all_gather | solution.py:71
  76.3 2.2 %convolution_convert_fusion.4 = bf16[128,2048]{1,0:T(8,128)(2,1)S(1)} fusion(bf16[128,384]{1,0:T(8,128)(2,1)} %multiply_convert_fusion.4, bf16[1,2048,384]{2,1,0:T(8,128)(2,1)} %all-gather.7.cloned.1.call-done), kind=kOutput, calls=%fused_computation.24 | convolution fusion | flops 201588736 | bytes 2195456 | tf_op jit(solution)/shard_map/dot_general | solution.py:25
  78.5 1.5 collective-permute-start.1
  80.0 2.5 %fusion.6 = f32[128,768]{1,0:T(8,128)S(1)} fusion(bf16[128,2048]{1,0:T(8,128)(2,1)S(1)} %gather_fusion, bf16[1,2048,768]{2,1,0:T(8,128)(2,1)} %all-gather.5.cloned.1.call-done), kind=kOutput, calls=%fused_computation.19 | convolution fusion | flops 402653184 | bytes 4063232 | tf_op jit(solution)/shard_map/dot_general | solution.py:32
  83.7 1.0 convolution_convert_fusion.1
  84.8 8.7 %collective-permute-done.1 = bf16[128,2048]{1,0:T(8,128)(2,1)S(1)} collective-permute-done((bf16[128,2048]{1,0:T(8,128)(2,1)S(1)}, bf16[128,2048]{1,0:T(8,128)(2,1)S(1)}, u32[]{:S(2)}, u32[]{:S(2)}) %collective-permute-start.1) | collective-permute-done | bytes 524320 | tf_op jit(solution)/shard_map/ppermute | solution.py:10
  93.8 1.7 collective-permute-start.2
  96.4 10.9 %collective-permute-done.2 = bf16[128,2048]{1,0:T(8,128)(2,1)S(1)} collective-permute-done((bf16[128,2048]{1,0:T(8,128)(2,1)S(1)}, bf16[128,2048]{1,0:T(8,128)(2,1)S(1)}, u32[]{:S(2)}, u32[]{:S(2)}) %collective-permute-start.2) | collective-permute-done | bytes 524320 | tf_op jit(solution)/shard_map/ppermute | solution.py:10
  108.3 1.0 convolution_convert_fusion
  110.3 4.5 %add_convert_fusion = bf16[2048,1152]{0,1:T(8,128)(2,1)} fusion(bf16[2048,1152]{0,1:T(8,128)(2,1)S(1)} %pad_maximum_fusion.1, bf16[2048,1152]{0,1:T(8,128)(2,1)S(1)} %pad_maximum_fusion), kind=kLoop, calls=%fused_computation.8 | loop fusion | flops 9437184 | bytes 14155776 | tf_op jit(solution)/shard_map/convert_element_type | solution.py:117
  115.7 4.0 %fusion.2 = f32[128,2048]{1,0:T(8,128)} fusion(bf16[1,2048,768]{2,1,0:T(8,128)(2,1)} %all-gather.5.cloned.1.call-done, bf16[128,384]{1,0:T(8,128)(2,1)S(1)} %copy-done.14, bf16[128,384]{1,0:T(8,128)(2,1)S(1)} %copy-done.12), kind=kOutput, calls=%fused_computation.15 | convolution fusion | flops 403046400 | bytes 4390912 | tf_op jit(solution)/shard_map/dot_general | solution.py:25
  119.7 4.1 %scatter_custom_fusion.2 = f32[128,2048]{1,0:T(8,128)} fusion(s32[128]{0:T(128)} %copy-done.22, f32[128,2048]{1,0:T(8,128)} %fusion.2, f32[]{:T(128)} %constant.31.clone.1), kind=kCustom, calls=%fused_computation.48 | custom fusion | flops 262144 | bytes 1049088 | tf_op jit(solution)/shard_map/scatter-add | solution.py:108
  123.8 3.8 %fusion.8 = bf16[128,2048]{1,0:T(8,128)(2,1)} fusion(bf16[1,2048,768]{2,1,0:T(8,128)(2,1)} %all-gather.5.cloned.1.call-done, bf16[128,384]{1,0:T(8,128)(2,1)S(1)} %copy-done.18, bf16[128,384]{1,0:T(8,128)(2,1)S(1)} %copy-done.16), kind=kOutput, calls=%fused_computation.23 | convolution fusion | flops 403308544 | bytes 3866624 | tf_op jit(solution)/shard_map/dot_general | solution.py:25
  127.6 1.4 collective-permute-start.3
  129.1 1.6 fusion.20
  130.7 3.3 %scatter_custom_fusion = f32[128,2048]{1,0:T(8,128)S(1)} fusion(s32[128]{0:T(128)} %copy-done.22, f32[128,2048]{1,0:T(8,128)} %get-tuple-element.31, f32[128]{0:T(128)S(1)} %and_select_fusion.4, f32[]{:T(128)} %constant.31.clone.1), kind=kCustom, calls=%fused_computation.44 | custom fusion | flops 524288 | bytes 2098176 | tf_op jit(solution)/shard_map/scatter-add | solution.py:107
  134.0 1.2 and_select_fusion
  136.0 3.2 %scatter_custom_fusion.1 = f32[128,2048]{1,0:T(8,128)S(1)} fusion(f32[128,2048]{1,0:T(8,128)S(1)} %scatter_custom_fusion, s32[128]{0:T(128)S(1)} %fusion.37, bf16[128,2048]{1,0:T(8,128)(2,1)} %copy-done.7, f32[128]{0:T(128)S(1)} %and_select_fusion.3), kind=kCustom, calls=%fused_computation.37 | custom fusion | flops 786432 | bytes 1573376 | tf_op jit(solution)/shard_map/scatter-add | solution.py:107
  140.0 1.0 collective-permute-done.3
  141.0 3.1 %scatter_custom_fusion.3 = f32[128,2048]{1,0:T(8,128)S(1)} fusion(f32[128,2048]{1,0:T(8,128)S(1)} %copy-done.5, s32[128]{0:T(128)S(1)} %fusion.37, bf16[128,2048]{1,0:T(8,128)(2,1)} %collective-permute-done.3), kind=kCustom, calls=%fused_computation.42 | custom fusion | flops 524288 | bytes 1572864 | tf_op jit(solution)/shard_map/scatter-add | solution.py:108
  145.0 24.5 %reduce-scatter.2.cloned.1.call-done = bf16[256,1152]{0,1:T(8,128)(2,1)} async-done(((bf16[2048,1152]{0,1:T(8,128)(2,1)}), bf16[256,1152]{0,1:T(8,128)(2,1)}) %reduce-scatter.2.cloned.1.call-update) | async-done | bytes 589840 | tf_op jit(solution)/shard_map/reduce_scatter | solution.py:116
  169.5 1.0 slice_bitcast_fusion
  170.5 0.9 copy.14
  171.4 0.9 slice_bitcast_fusion.1
  (91 shorter events, 14.3 us)
Async XLA Ops:
  7.2 2.4 %copy-start = (bf16[128,2048]{1,0:T(8,128)(2,1)S(1)}, bf16[128,2048]{1,0:T(8,128)(2,1)}, u32[]{:S(2)}) copy-start(bf16[128,2048]{1,0:T(8,128)(2,1)} %param.7) | copy-start | bytes 1572868
  7.2 43.5 %all-gather.5.cloned.1.call-start = ((), (), s32[]{:S(2)}) async-start(), calls=%async_computation.2 | async-start | bytes 3538944 | tf_op jit(solution)/shard_map/all_gather | solution.py:70
  7.9 68.3 %all-gather.7.cloned.1.call-start = ((), (), s32[]{:S(2)}) async-start(), calls=%async_computation.3 | async-start | bytes 1769472 | tf_op jit(solution)/shard_map/all_gather | solution.py:71
  8.7 160.8 %reduce-scatter.2.cloned.1.call-start = ((), (), s32[]{:S(2)}) async-start(), calls=%async_computation.1 | async-start | bytes 5308416 | tf_op jit(solution)/shard_map/reduce_scatter | solution.py:116
  10.5 5.0 %copy-start.1 = (bf16[128,2048]{1,0:T(8,128)(2,1)S(1)}, bf16[128,2048]{1,0:T(8,128)(2,1)}, u32[]{:S(2)}) copy-start(bf16[128,2048]{1,0:T(8,128)(2,1)} %param.8) | copy-start | bytes 1572868
  10.5 15.1 %collective-permute-start = (bf16[128,2048]{1,0:T(8,128)(2,1)S(1)}, bf16[128,2048]{1,0:T(8,128)(2,1)S(1)}, u32[]{:S(2)}, u32[]{:S(2)}) collective-permute-start(bf16[128,2048]{1,0:T(8,128)(2,1)S(1)} %gather_fusion.1), channel_id=1, source_target_pairs={{8,0},{16,8},{24,16},{0,24},{9,1},{17,9},{25,17},{1,25},{10,2},{18... | collective-permute-start | bytes 1572872 | tf_op jit(solution)/shard_map/ppermute | solution.py:10
  14.6 1.0 copy-start.22
  16.5 1.8 copy-start.19
  16.5 2.4 %copy-start.20 = (f32[1,4,64]{2,1,0:T(4,128)S(1)}, f32[1,4,64]{2,1,0:T(4,128)}, u32[]{:S(2)}) copy-start(f32[1,4,64]{2,1,0:T(4,128)} %param.12) | copy-start | bytes 3076
  16.5 2.6 %copy-start.21 = (s32[1,2]{1,0:T(1,128)S(1)}, s32[1,2]{1,0:T(1,128)}, u32[]{:S(2)}) copy-start(s32[1,2]{1,0:T(1,128)} %param.13) | copy-start | bytes 28
  18.3 7.4 %copy-start.25 = (pred[1,2,64]{2,1,0:T(4,128)(4,1)}, pred[1,2,64]{2,1,0:T(4,128)(4,1)S(1)}, u32[]{:S(2)}) copy-start(pred[1,2,64]{2,1,0:T(4,128)(4,1)S(1)} %get-tuple-element.22) | copy-start | bytes 388
  25.7 28.2 %copy-start.3 = (bf16[128,2048]{1,0:T(8,128)(2,1)}, bf16[128,2048]{1,0:T(8,128)(2,1)S(1)}, u32[]{:S(2)}) copy-start(bf16[128,2048]{1,0:T(8,128)(2,1)S(1)} %collective-permute-done) | copy-start | bytes 1572868
  76.3 6.2 %copy-start.2 = (bf16[1,2048,384]{2,1,0:T(8,128)(2,1)S(1)}, bf16[1,2048,384]{2,1,0:T(8,128)(2,1)}, u32[]{:S(2)}) copy-start(bf16[1,2048,384]{2,1,0:T(8,128)(2,1)} %all-gather.7.cloned.1.call-done) | copy-start | bytes 4718596
  78.5 15.0 %collective-permute-start.1 = (bf16[128,2048]{1,0:T(8,128)(2,1)S(1)}, bf16[128,2048]{1,0:T(8,128)(2,1)S(1)}, u32[]{:S(2)}, u32[]{:S(2)}) collective-permute-start(bf16[128,2048]{1,0:T(8,128)(2,1)S(1)} %convolution_convert_fusion.4), channel_id=1, source_target_pairs={{24,0},{0,8},{8,16},{16,24},{25,1},{1,9},{9,17},{17,25},{26,2},{2,... | collective-permute-start | bytes 1572872 | tf_op jit(solution)/shard_map/ppermute | solution.py:10
  83.0 0.7 copy-start.9
  83.0 1.7 copy-start.11
  83.0 1.7 copy-start.13
  83.7 9.8 %copy-start.6 = (bf16[128,2048]{1,0:T(8,128)(2,1)S(1)}, bf16[128,2048]{1,0:T(8,128)(2,1)}, u32[]{:S(2)}) copy-start(bf16[128,2048]{1,0:T(8,128)(2,1)} %gather_fusion.3) | copy-start | bytes 1572868
  93.5 2.9 %copy-start.7 = (bf16[128,2048]{1,0:T(8,128)(2,1)}, bf16[128,2048]{1,0:T(8,128)(2,1)S(1)}, u32[]{:S(2)}) copy-start(bf16[128,2048]{1,0:T(8,128)(2,1)S(1)} %collective-permute-done.1) | copy-start | bytes 1572868
  93.8 13.5 %collective-permute-start.2 = (bf16[128,2048]{1,0:T(8,128)(2,1)S(1)}, bf16[128,2048]{1,0:T(8,128)(2,1)S(1)}, u32[]{:S(2)}, u32[]{:S(2)}) collective-permute-start(bf16[128,2048]{1,0:T(8,128)(2,1)S(1)} %get-tuple-element.20), channel_id=1, source_target_pairs={{8,0},{16,8},{24,16},{0,24},{9,1},{17,9},{25,17},{1,25},{10,2},{18... | collective-permute-start | bytes 1572872 | tf_op jit(solution)/shard_map/ppermute | solution.py:10
  96.3 11.3 %copy-start.8 = (bf16[128,384]{1,0:T(8,128)(2,1)S(1)}, bf16[128,384]{1,0:T(8,128)(2,1)}, u32[]{:S(2)}) copy-start(bf16[128,384]{1,0:T(8,128)(2,1)} %multiply_convert_fusion.4) | copy-start | bytes 294916
  96.4 12.0 %copy-start.4 = (bf16[128,2048]{1,0:T(8,128)(2,1)S(1)}, bf16[128,2048]{1,0:T(8,128)(2,1)}, u32[]{:S(2)}) copy-start(bf16[128,2048]{1,0:T(8,128)(2,1)} %copy-done.3) | copy-start | bytes 1572868
  107.7 1.7 copy-start.15
  107.7 1.7 copy-start.17
  114.8 0.8 copy-start.24
  114.8 0.9 copy-start.12
  114.8 0.9 copy-start.14
  115.4 8.4 %copy-start.16 = (bf16[128,384]{1,0:T(8,128)(2,1)S(1)}, bf16[128,384]{1,0:T(8,128)(2,1)}, u32[]{:S(2)}) copy-start(bf16[128,384]{1,0:T(8,128)(2,1)} %copy-done.15) | copy-start | bytes 294916
  115.4 8.4 %copy-start.18 = (bf16[128,384]{1,0:T(8,128)(2,1)S(1)}, bf16[128,384]{1,0:T(8,128)(2,1)}, u32[]{:S(2)}) copy-start(bf16[128,384]{1,0:T(8,128)(2,1)} %copy-done.17) | copy-start | bytes 294916
  119.7 9.4 %copy-start.10 = (bf16[128,384]{1,0:T(8,128)(2,1)S(1)}, bf16[128,384]{1,0:T(8,128)(2,1)}, u32[]{:S(2)}) copy-start(bf16[128,384]{1,0:T(8,128)(2,1)} %copy-done.9) | copy-start | bytes 294916
  127.6 13.3 %collective-permute-start.3 = (bf16[128,2048]{1,0:T(8,128)(2,1)}, bf16[128,2048]{1,0:T(8,128)(2,1)}, u32[]{:S(2)}, u32[]{:S(2)}) collective-permute-start(bf16[128,2048]{1,0:T(8,128)(2,1)} %fusion.8), channel_id=1, source_target_pairs={{24,0},{0,8},{8,16},{16,24},{25,1},{1,9},{9,17},{17,25},{26,2},{2,... | collective-permute-start | bytes 1572872 | tf_op jit(solution)/shard_map/ppermute | solution.py:10
  130.7 10.3 %copy-start.5 = (f32[128,2048]{1,0:T(8,128)S(1)}, f32[128,2048]{1,0:T(8,128)}, u32[]{:S(2)}) copy-start(f32[128,2048]{1,0:T(8,128)} %scatter_custom_fusion.2) | copy-start | bytes 3145732
  (2 other events, 1.2 us)
Sparse Core Ops, SparseCore 0:
  9.7 40.9 all-gather.4
  52.3 23.9 all-gather.6
  114.9 54.4 reduce-scatter.1
where the time goes:
time: 180 us
  waiting for transfers between devices  98.6 us (55%)
  other arithmetic  25.2 us (14%)
  matrix products  20.8 us (12%)
  between operations  14.1 us (8%)
  local copies, waits for them, and re-layouts  12.2 us (7%)
  starting transfers between devices  8.73 us (5%)
    ppermute x4, waiting for transfers between devices, shifted(): return lax.ppermute(block, axis, route)  25.3 us
    all_gather x1, waiting for transfers between devices, body(): lax.all_gather(w_in[0], 'dp', axis=0, tiled=True)  25 us
    reduce_scatter x1, waiting for transfers between devices, body(): lax.psum_scatter(total_term.astype(jnp.bfloat16), 'dp', scatter_dimension...  24.5 us
    all_gather x1, waiting for transfers between devices, body(): lax.all_gather(w_out[0], 'dp', axis=0, tiled=True)  22.4 us
    dot_general x4, matrix products, contract_cols(): lax.dot_general(left_mat, right_mat, (((1,), (1,)), ((), ())), preferred_...  11.6 us
    ppermute x4, starting transfers between devices, shifted(): return lax.ppermute(block, axis, route)  8.62 us
    scatter-add x2, other arithmetic, body(): token_sum = token_sum.at[token_ids].add(input_grad)  7.21 us
    scatter-add x2, other arithmetic, body(): mixed_sum = mixed_sum.at[token_ids].add(weight[:, None] * output)  6.51 us
  transfers between devices with their start and end apart: 7, of which 7 were waited for; matrix products, arithmetic and copies ran while one was open for 24% of the time, Pallas kernels for 0%

commit v1 on v0

v1 whole, which is shorter than its diff:
```python
import jax
import jax.numpy as jnp
from jax import lax
from jax.sharding import PartitionSpec as P


def shifted(block, axis, distance):
    devices = range(lax.axis_size(axis))
    route = [((i - distance) % len(devices), i) for i in devices]
    return lax.ppermute(block, axis, route)


def contract_rows(left_mat, right_mat):
    return lax.dot_general(
        left_mat, right_mat, (((0,), (0,)), ((), ())), preferred_element_type=jnp.float32
    )


def contract_cols(left_mat, right_mat):
    return lax.dot_general(
        left_mat, right_mat, (((1,), (1,)), ((), ())), preferred_element_type=jnp.float32
    )


def body(tokens, cotangent, w_in, w_out, block_rows, block_gates, block_count):
    stops = block_count.shape[1]
    block_size = block_rows.shape[2]
    span = block_rows.shape[1] // stops * block_size
    rows = tokens.shape[0]
    ffw = w_out.shape[2]
    bf16, f32 = jnp.bfloat16, jnp.float32
    entries = block_rows.reshape(stops, span)
    gates = block_gates.reshape(stops, span)
    counts = block_count[0]
    positions = jnp.arange(span, dtype=jnp.int32)
    live = (positions[None, :] // block_size < counts[:, None]) & (entries >= 0)
    pick = (
        live[:, :, None] & (entries[:, :, None] == jnp.arange(rows, dtype=jnp.int32))
    ).astype(f32)
    gate_of = jnp.sum(pick * gates[:, :, None], axis=1)

    slab_in = lax.all_gather(w_in[0], "dp", axis=0, tiled=True)
    slab_out = lax.all_gather(w_out[0], "dp", axis=0, tiled=True)
    xs, cs, gs = [tokens], [cotangent], [gate_of[0]]
    for k in range(1, stops):
        x, c, g = shifted((tokens, cotangent, gate_of[k]), "expert", -k)
        xs.append(x)
        cs.append(c)
        gs.append(g)
    x, c, g = jnp.concatenate(xs), jnp.concatenate(cs), jnp.concatenate(gs)[:, None]
    pre = jnp.dot(x, slab_in, preferred_element_type=f32)
    h, u = pre[:, :ffw], pre[:, ffw:]
    dc = jnp.dot(c, slab_out, preferred_element_type=f32)
    sig = jax.nn.sigmoid(h)
    act = h * sig
    a = act * u
    gate_tok = jnp.sum(a * dc, axis=1)
    da = g * dc
    ag = (g * a).astype(bf16)
    hg = jnp.concatenate([da * u * (sig * (1.0 + h * (1.0 - sig))), da * act], axis=1).astype(bf16)
    o = contract_cols(ag, slab_out)
    tg = contract_cols(hg, slab_in)
    mixed, token_grad, gate_parts = o[:rows], tg[:rows], [gate_tok[:rows]]
    for k in range(1, stops):
        cut = slice(k * rows, (k + 1) * rows)
        po, pt, pg = shifted((o[cut].astype(bf16), tg[cut].astype(bf16), gate_tok[cut]), "expert", k)
        mixed = mixed + po.astype(f32)
        token_grad = token_grad + pt.astype(f32)
        gate_parts.append(pg)
    term = jnp.concatenate([contract_rows(x, hg), contract_rows(c, ag)], axis=1).astype(bf16)
    total = lax.psum_scatter(term, "dp", scatter_dimension=0, tiled=True)
    gate_grad = jnp.sum(pick * jnp.stack(gate_parts)[:, None, :], axis=2).reshape(block_rows.shape)
    return (
        mixed.astype(bf16),
        token_grad.astype(bf16),
        gate_grad,
        total[:, : 2 * ffw][None],
        total[:, 2 * ffw :][None],
    )


def solution(mesh):
    in_specs = (
        P(("expert", "dp"), None),
        P(("expert", "dp"), None),
        P("expert", "dp", None),
        P("expert", "dp", None),
        P(("expert", "dp"), None, None),
        P(("expert", "dp"), None, None),
        P(("expert", "dp"), None),
    )
    out_specs = (
        P(("expert", "dp"), None),
        P(("expert", "dp"), None),
        P(("expert", "dp"), None, None),
        P("expert", "dp", None),
        P("expert", "dp", None),
    )
    return jax.shard_map(body, mesh=mesh, in_specs=in_specs, out_specs=out_specs, check_vma=False)
```

time: 180 us -> 158 us (0.88)
  other arithmetic: 25.2 us -> 8.28 us
  matrix products: 20.8 us -> 9.09 us
  waiting for transfers between devices: 98.6 us -> 105 us
  starting transfers between devices: 8.73 us -> 10.6 us
    ppermute x4 -> x6, waiting for transfers between devices: 25.3 us -> 41.4 us  [shifted(): return lax.ppermute(block, axis, route)]
    scatter-add x4 -> x0, other arithmetic: 13.7 us -> none  [the longest x2 7.21 us: body(): token_sum = token_sum.at[token_ids].add(input_grad)]
    dot_general x4 -> x2, matrix products: 11.6 us -> 1.74 us  [contract_cols(): lax.dot_general(left_mat, right_mat, (((1,), (1,)), ((), ())), preferred_...]
    all_gather x2, waiting for transfers between devices: 47.4 us -> 37.9 us  [the longest x1 22.7 us: body(): slab_out = lax.all_gather(w_out[0], 'dp', axis=0, tiled=True)]
    gather x4 -> x0, local copies, waits for them, and re-layouts: 4.53 us -> none  [the longest x2 2.66 us: body(): cot_rows = cotangent[token_ids]]
    unnamed x56 -> x18, local copies, waits for them, and re-layouts: 3.03 us -> 7.07 us
    convert_element_type x4 -> x2, other arithmetic: 6.93 us -> 4.2 us  [the longest x1 2.26 us: body(): token_grad.astype(bf16)]
    mul x3 -> x0, other arithmetic: 2.5 us -> none  [the longest x2 1.25 us: body(): weight = gate_table[station] * live_mask]
  transfers between devices with their start and end apart: 7 -> 9, of which waited for: 7 -> 9; matrix products, arithmetic and copies ran while one was open for 24% -> 8% of each run, Pallas kernels for 0% -> 0%
where the time goes in v1:
time: 158 us
  waiting for transfers between devices  105 us (66%)
  between operations  13.9 us (9%)
  local copies, waits for them, and re-layouts  10.7 us (7%)
  starting transfers between devices  10.6 us (7%)
  matrix products  9.09 us (6%)
  other arithmetic  8.28 us (5%)
    ppermute x6, waiting for transfers between devices, shifted(): return lax.ppermute(block, axis, route)  41.4 us
    reduce_scatter x1, waiting for transfers between devices, body(): total = lax.psum_scatter(term, 'dp', scatter_dimension=0, tiled=True)  24.5 us
    all_gather x1, waiting for transfers between devices, body(): slab_out = lax.all_gather(w_out[0], 'dp', axis=0, tiled=True)  22.7 us
    all_gather x1, waiting for transfers between devices, body(): slab_in = lax.all_gather(w_in[0], 'dp', axis=0, tiled=True)  15.2 us
    ppermute x6, starting transfers between devices, shifted(): return lax.ppermute(block, axis, route)  10.5 us
    unnamed x18, local copies, waits for them, and re-layouts  7.07 us
  transfers between devices with their start and end apart: 9, of which 9 were waited for; matrix products, arithmetic and copies ran while one was open for 8% of the time, Pallas kernels for 0%

profile of v1, /device:TPU:0, one launch (start us, length us, event | category | flops | bytes accessed | tf_op | source)
XLA Modules:
  0.0 157.8 jit_solution(18397176287086914564)
XLA Ops:
  8.7 3.9 %collective-permute-start.1 = (bf16[128,2048]{1,0:T(8,128)(2,1)}, bf16[128,2048]{1,0:T(8,128)(2,1)S(1)}, u32[]{:S(2)}, u32[]{:S(2)}) collective-permute-start(bf16[128,2048]{1,0:T(8,128)(2,1)} %param.7), channel_id=1, source_target_pairs={{8,0},{16,8},{24,16},{0,24},{9,1},{17,9},{25,17},{1,25},{10,2},{18... | collective-permute-start | bytes 1572872 | tf_op jit(solution)/shard_map/ppermute | solution.py:10
  13.2 1.1 constant_dynamic-update-slice_fusion.1
  14.3 0.8 reshape.94
  15.0 1.1 constant_dynamic-update-slice_fusion.3
  16.1 9.2 %collective-permute-done.1 = bf16[128,2048]{1,0:T(8,128)(2,1)S(1)} collective-permute-done((bf16[128,2048]{1,0:T(8,128)(2,1)}, bf16[128,2048]{1,0:T(8,128)(2,1)S(1)}, u32[]{:S(2)}, u32[]{:S(2)}) %collective-permute-start.1) | collective-permute-done | bytes 524320 | tf_op jit(solution)/shard_map/ppermute | solution.py:10
  25.3 10.0 %collective-permute-done.3 = bf16[128,2048]{1,0:T(8,128)(2,1)S(1)} collective-permute-done((bf16[128,2048]{1,0:T(8,128)(2,1)}, bf16[128,2048]{1,0:T(8,128)(2,1)S(1)}, u32[]{:S(2)}, u32[]{:S(2)}) %collective-permute-start.3) | collective-permute-done | bytes 524320 | tf_op jit(solution)/shard_map/ppermute | solution.py:10
  35.4 15.2 %all-gather.5.cloned.1.call-done = bf16[1,2048,768]{2,1,0:T(8,128)(2,1)} async-done(((bf16[1,256,768]{2,1,0:T(8,128)(2,1)}), bf16[1,2048,768]{2,1,0:T(8,128)(2,1)}) %all-gather.5.cloned.1.call-update) | async-done | bytes 3145744 | tf_op jit(solution)/shard_map/all_gather | solution.py:42
  50.7 2.9 %fusion.2 = f32[256,768]{1,0:T(8,128)S(1)} fusion(bf16[256,2048]{1,0:T(8,128)(2,1)S(1)} %constant_dynamic-update-slice_fusion, bf16[1,2048,768]{2,1,0:T(8,128)(2,1)} %all-gather.5.cloned.1.call-done), kind=kOutput, calls=%fused_computation.4 | convolution fusion | flops 805306368 | bytes 4980736 | tf_op jit(solution)/shard_map/dot_general | solution.py:51
  53.6 22.7 %all-gather.7.cloned.1.call-done = bf16[1,2048,384]{2,1,0:T(8,128)(2,1)} async-done(((bf16[1,256,384]{2,1,0:T(8,128)(2,1)}), bf16[1,2048,384]{2,1,0:T(8,128)(2,1)}) %all-gather.7.cloned.1.call-update) | async-done | bytes 1572880 | tf_op jit(solution)/shard_map/all_gather | solution.py:43
  76.2 2.9 %multiply_reduce_fusion = (f32[256]{0:T(256)S(1)}, f32[256,384]{1,0:T(8,128)}) fusion(f32[256,768]{1,0:T(8,128)S(1)} %fusion.2, bf16[256,2048]{1,0:T(8,128)(2,1)S(1)} %constant_dynamic-update-slice_fusion.2, bf16[1,2048,384]{2,1,0:T(8,128)(2,1)} %all-gather.7.cloned.1.call-done), kind=kOutput, calls=%fused_computation.19 | convolution fusion | flops 403341056 | bytes 3802112 | tf_op jit(solution)/shard_map/dot_general | solution.py:53
  79.1 1.5 collective-permute-start.5
  80.8 2.8 %collective-permute-done.5 = f32[128]{0:T(128)S(1)} collective-permute-done((f32[128]{0:T(128)S(1)}, f32[128]{0:T(128)S(1)}, u32[]{:S(2)}, u32[]{:S(2)}) %collective-permute-start.5) | collective-permute-done | bytes 544 | tf_op jit(solution)/shard_map/ppermute | solution.py:10
  83.8 1.5 collective-permute-start
  85.3 2.1 %collective-permute-done = f32[128]{0:T(128)S(1)} collective-permute-done((f32[128]{0:T(128)S(1)}, f32[128]{0:T(128)S(1)}, u32[]{:S(2)}, u32[]{:S(2)}) %collective-permute-start) | collective-permute-done | bytes 544 | tf_op jit(solution)/shard_map/ppermute | solution.py:10
  87.4 1.3 multiply_convert_fusion.1
  89.3 1.0 convolution_convert_fusion
  90.3 2.5 %pad_maximum_fusion = bf16[2048,1152]{0,1:T(8,128)(2,1)} fusion(bf16[2048,384]{0,1:T(8,128)(2,1)S(1)} %convolution_convert_fusion.1, bf16[2048,768]{0,1:T(8,128)(2,1)S(1)} %convolution_convert_fusion), kind=kLoop, calls=%fused_computation | loop fusion | flops 9437184 | bytes 9437184 | tf_op jit(solution)/shard_map/concatenate | solution.py:70
  92.9 1.9 %copy-done.1 = bf16[1,2048,768]{2,1,0:T(8,128)(2,1)S(1)} copy-done((bf16[1,2048,768]{2,1,0:T(8,128)(2,1)S(1)}, bf16[1,2048,768]{2,1,0:T(8,128)(2,1)}, u32[]{:S(2)}) %copy-start.1) | copy-done | bytes 3145752
  94.7 1.0 fusion
  95.8 1.3 copy-done
  97.1 1.5 collective-permute-start.4
  98.6 0.7 fusion.6
  99.4 1.5 collective-permute-start.2
  101.6 11.4 %collective-permute-done.4 = bf16[128,2048]{1,0:T(8,128)(2,1)} collective-permute-done((bf16[128,2048]{1,0:T(8,128)(2,1)S(1)}, bf16[128,2048]{1,0:T(8,128)(2,1)}, u32[]{:S(2)}, u32[]{:S(2)}) %collective-permute-start.4) | collective-permute-done | bytes 524320 | tf_op jit(solution)/shard_map/ppermute | solution.py:10
  113.0 2.3 %fusion.8 = bf16[128,2048]{1,0:T(8,128)(2,1)} fusion(f32[256,2048]{1,0:T(8,128)} %copy-done, bf16[128,2048]{1,0:T(8,128)(2,1)} %collective-permute-done.4), kind=kLoop, calls=%fused_computation.13 | loop fusion | flops 786432 | bytes 2097152 | tf_op jit(solution)/shard_map/convert_element_type | solution.py:75
  115.2 5.9 %collective-permute-done.2 = bf16[128,2048]{1,0:T(8,128)(2,1)} collective-permute-done((bf16[128,2048]{1,0:T(8,128)(2,1)S(1)}, bf16[128,2048]{1,0:T(8,128)(2,1)}, u32[]{:S(2)}, u32[]{:S(2)}) %collective-permute-start.2) | collective-permute-done | bytes 524320 | tf_op jit(solution)/shard_map/ppermute | solution.py:10
  121.1 1.9 %fusion.9 = bf16[128,2048]{1,0:T(8,128)(2,1)} fusion(f32[256,2048]{1,0:T(8,128)S(1)} %fusion.6, bf16[128,2048]{1,0:T(8,128)(2,1)} %collective-permute-done.2), kind=kLoop, calls=%fused_computation.16 | loop fusion | flops 786432 | bytes 2097152 | tf_op jit(solution)/shard_map/convert_element_type | solution.py:74
  123.1 24.5 %reduce-scatter.2.cloned.1.call-done = bf16[256,1152]{0,1:T(8,128)(2,1)} async-done(((bf16[2048,1152]{0,1:T(8,128)(2,1)}), bf16[256,1152]{0,1:T(8,128)(2,1)}) %reduce-scatter.2.cloned.1.call-update) | async-done | bytes 589840 | tf_op jit(solution)/shard_map/reduce_scatter | solution.py:71
  147.5 1.0 slice_bitcast_fusion
  148.5 0.9 copy.14
  149.5 0.9 slice_bitcast_fusion.1
  150.4 0.8 copy.15
  (33 shorter events, 4.0 us)
Async XLA Ops:
  7.2 43.5 %all-gather.5.cloned.1.call-start = ((), (), s32[]{:S(2)}) async-start(), calls=%async_computation.2 | async-start | bytes 3538944 | tf_op jit(solution)/shard_map/all_gather | solution.py:42
  7.9 68.3 %all-gather.7.cloned.1.call-start = ((), (), s32[]{:S(2)}) async-start(), calls=%async_computation.3 | async-start | bytes 1769472 | tf_op jit(solution)/shard_map/all_gather | solution.py:43
  8.6 138.9 %reduce-scatter.2.cloned.1.call-start = ((), (), s32[]{:S(2)}) async-start(), calls=%async_computation.1 | async-start | bytes 5308416 | tf_op jit(solution)/shard_map/reduce_scatter | solution.py:71
  8.7 16.6 %collective-permute-start.1 = (bf16[128,2048]{1,0:T(8,128)(2,1)}, bf16[128,2048]{1,0:T(8,128)(2,1)S(1)}, u32[]{:S(2)}, u32[]{:S(2)}) collective-permute-start(bf16[128,2048]{1,0:T(8,128)(2,1)} %param.7), channel_id=1, source_target_pairs={{8,0},{16,8},{24,16},{0,24},{9,1},{17,9},{25,17},{1,25},{10,2},{18... | collective-permute-start | bytes 1572872 | tf_op jit(solution)/shard_map/ppermute | solution.py:10
  12.6 22.7 %collective-permute-start.3 = (bf16[128,2048]{1,0:T(8,128)(2,1)}, bf16[128,2048]{1,0:T(8,128)(2,1)S(1)}, u32[]{:S(2)}, u32[]{:S(2)}) collective-permute-start(bf16[128,2048]{1,0:T(8,128)(2,1)} %param.8), channel_id=1, source_target_pairs={{8,0},{16,8},{24,16},{0,24},{9,1},{17,9},{25,17},{1,25},{10,2},{18... | collective-permute-start | bytes 1572872 | tf_op jit(solution)/shard_map/ppermute | solution.py:10
  53.5 27.1 %copy-start.6 = (s32[1,2]{1,0:T(1,128)S(1)}, s32[1,2]{1,0:T(1,128)}, u32[]{:S(2)}) copy-start(s32[1,2]{1,0:T(1,128)} %param.13) | copy-start | bytes 28
  53.5 27.1 %copy-start.5 = (f32[1,4,64]{2,1,0:T(4,128)S(1)}, f32[1,4,64]{2,1,0:T(4,128)}, u32[]{:S(2)}) copy-start(f32[1,4,64]{2,1,0:T(4,128)} %param.12) | copy-start | bytes 3076
  79.1 4.4 %collective-permute-start.5 = (f32[128]{0:T(128)S(1)}, f32[128]{0:T(128)S(1)}, u32[]{:S(2)}, u32[]{:S(2)}) collective-permute-start(f32[128]{0:T(128)S(1)} %get-tuple-element.23), channel_id=1, source_target_pairs={{24,0},{0,8},{8,16},{16,24},{25,1},{1,9},{9,17},{17,25},{26,2},{2,... | collective-permute-start | bytes 1544 | tf_op jit(solution)/shard_map/ppermute | solution.py:10
  83.8 3.6 %collective-permute-start = (f32[128]{0:T(128)S(1)}, f32[128]{0:T(128)S(1)}, u32[]{:S(2)}, u32[]{:S(2)}) collective-permute-start(f32[128]{0:T(128)S(1)} %get-tuple-element.21), channel_id=1, source_target_pairs={{8,0},{16,8},{24,16},{0,24},{9,1},{17,9},{25,17},{1,25},{10,2},{18... | collective-permute-start | bytes 1544 | tf_op jit(solution)/shard_map/ppermute | solution.py:10
  88.7 1.7 %copy-start.2 = (bf16[256,384]{1,0:T(8,128)(2,1)}, bf16[256,384]{1,0:T(8,128)(2,1)S(1)}, u32[]{:S(2)}) copy-start(bf16[256,384]{1,0:T(8,128)(2,1)S(1)} %get-tuple-element.19) | copy-start | bytes 589828
  92.8 1.9 %copy-start.1 = (bf16[1,2048,768]{2,1,0:T(8,128)(2,1)S(1)}, bf16[1,2048,768]{2,1,0:T(8,128)(2,1)}, u32[]{:S(2)}) copy-start(bf16[1,2048,768]{2,1,0:T(8,128)(2,1)} %all-gather.5.cloned.1.call-done) | copy-start | bytes 9437188
  94.7 3.9 %copy-start.3 = (bf16[256,384]{1,0:T(8,128)(2,1)S(1)}, bf16[256,384]{1,0:T(8,128)(2,1)}, u32[]{:S(2)}) copy-start(bf16[256,384]{1,0:T(8,128)(2,1)} %copy-done.2) | copy-start | bytes 589828
  94.7 3.9 %copy-start.4 = (bf16[1,2048,384]{2,1,0:T(8,128)(2,1)S(1)}, bf16[1,2048,384]{2,1,0:T(8,128)(2,1)}, u32[]{:S(2)}) copy-start(bf16[1,2048,384]{2,1,0:T(8,128)(2,1)} %all-gather.7.cloned.1.call-done) | copy-start | bytes 4718596
  95.7 1.4 copy-start
  97.1 15.9 %collective-permute-start.4 = (bf16[128,2048]{1,0:T(8,128)(2,1)S(1)}, bf16[128,2048]{1,0:T(8,128)(2,1)}, u32[]{:S(2)}, u32[]{:S(2)}) collective-permute-start(bf16[128,2048]{1,0:T(8,128)(2,1)S(1)} %slice.85), channel_id=1, source_target_pairs={{24,0},{0,8},{8,16},{16,24},{25,1},{1,9},{9,17},{17,25},{26,2},{2,... | collective-permute-start | bytes 1572872 | tf_op jit(solution)/shard_map/ppermute | solution.py:10
  99.4 21.7 %collective-permute-start.2 = (bf16[128,2048]{1,0:T(8,128)(2,1)S(1)}, bf16[128,2048]{1,0:T(8,128)(2,1)}, u32[]{:S(2)}, u32[]{:S(2)}) collective-permute-start(bf16[128,2048]{1,0:T(8,128)(2,1)S(1)} %slice.86), channel_id=1, source_target_pairs={{24,0},{0,8},{8,16},{16,24},{25,1},{1,9},{9,17},{17,25},{26,2},{2,... | collective-permute-start | bytes 1572872 | tf_op jit(solution)/shard_map/ppermute | solution.py:10
Sparse Core Ops, SparseCore 0:
  9.6 40.9 all-gather.4
  52.3 23.9 all-gather.6
  93.0 54.4 reduce-scatter.1

commit v2 on v1

v2 whole, which is shorter than its diff:
```python
import functools

import jax
import jax.numpy as jnp
from jax import lax
from jax.experimental import pallas as pl
from jax.experimental.pallas import tpu as pltpu
from jax.sharding import PartitionSpec as P

BF16, F32 = jnp.bfloat16, jnp.float32
MESH = pl.DeviceIdType.MESH
LANES = 128


def dot_nn(left, right):
    return jnp.dot(left, right, preferred_element_type=F32)


def dot_nt(left, right):
    return lax.dot_general(left, right, (((1,), (1,)), ((), ())), preferred_element_type=F32)


def kernel(
    dims,
    tok_ref,
    cot_ref,
    win_ref,
    wout_ref,
    meta_ref,
    mixed_ref,
    tgrad_ref,
    gate_ref,
    gin_ref,
    gout_ref,
    xa,
    ca,
    ma,
    w,
    xt,
    ct,
    xts,
    cts,
    hid,
    part,
    rbr,
    rbl,
    o0,
    t0,
    ob,
    tb,
    gb,
    ro,
    rt,
    rg,
    acc,
    s_agr,
    r_agr,
    s_agl,
    r_agl,
    s_sib,
    r_sib,
    s_xt,
    r_xt,
    s_hid,
    r_hid,
    s_rsr,
    r_rsr,
    s_rsl,
    r_rsl,
    s_tok,
    r_tok,
    s_ret,
    r_ret,
    s_rg,
    r_rg,
):
    n_exp, n_dp, stops = dims
    n = n_dp // 2
    rows, width = tok_ref.shape
    sr, ffw = wout_ref.shape
    qw = LANES
    nq = ffw // qw
    span = meta_ref.shape[2]
    td = next(t for t in (512, 256, 128) if width % t == 0)
    tiles = width // td

    e = lax.axis_index("expert")
    d = lax.axis_index("dp")
    z = d // 2
    c = d % 2
    has_l = z > 0
    has_r = z < n - 1
    right = {"expert": e, "dp": d + 2}
    left = {"expert": e, "dp": d - 2}
    sib = {"expert": e, "dp": 2 * z + (1 - c)}

    def cycle(k):
        return {"expert": (e + k) % n_exp, "dp": d}

    def remote(src, dst, ss, rs, dev):
        return pltpu.make_async_remote_copy(
            src_ref=src, dst_ref=dst, send_sem=ss, recv_sem=rs, device_id=dev, device_id_type=MESH
        )

    offsets = sorted({k % n_exp for k in range(1, stops)} | {-k % n_exp for k in range(1, stops)})
    barrier = pltpu.get_barrier_semaphore()
    pl.semaphore_signal(barrier, inc=1, device_id=sib, device_id_type=MESH)
    for k in offsets:
        pl.semaphore_signal(barrier, inc=1, device_id=cycle(k), device_id_type=MESH)

    @pl.when(has_l)
    def _():
        pl.semaphore_signal(barrier, inc=1, device_id=left, device_id_type=MESH)

    @pl.when(has_r)
    def _():
        pl.semaphore_signal(barrier, inc=1, device_id=right, device_id_type=MESH)

    own = pl.ds(pl.multiple_of(d * sr, 16), sr)
    for q in range(nq):
        w[q, own, 0:qw] = win_ref[:, q * qw : (q + 1) * qw]
        w[q, own, qw : 2 * qw] = win_ref[:, ffw + q * qw : ffw + (q + 1) * qw]
        w[q, own, 2 * qw : 3 * qw] = wout_ref[:, q * qw : (q + 1) * qw]
    neighbours = jnp.where(has_l, 1, 0) + jnp.where(has_r, 1, 0)
    pl.semaphore_wait(barrier, 1 + len(offsets) + neighbours)

    def shard(q, chip, core):
        return w.at[q, pl.ds(pl.multiple_of((2 * chip + core) * sr, 16), sr)]

    def ag_right(q, i):
        ref = shard(q, z - i, c)
        return remote(ref, ref, s_agr.at[q, i], r_agr.at[q, i], right)

    def ag_left(q, i):
        ref = shard(q, z + i, c)
        return remote(ref, ref, s_agl.at[q, i], r_agl.at[q, i], left)

    def from_left(q, i):
        ref = shard(q, z - 1 - i, c)
        return remote(ref, ref, s_agr.at[q, i], r_agr.at[q, i], left)

    def from_right(q, i):
        ref = shard(q, z + 1 + i, c)
        return remote(ref, ref, s_agl.at[q, i], r_agl.at[q, i], right)

    def ag_sib(q, chip, index, core):
        ref = shard(q, chip, core)
        return remote(ref, ref, s_sib.at[q, index], r_sib.at[q, index], sib)

    def tok_copies(k):
        cut = pl.ds(k * rows, rows)
        return [
            remote(tok_ref, xa.at[cut], s_tok.at[k, 0], r_tok.at[k, 0], cycle(-k)),
            remote(cot_ref, ca.at[cut], s_tok.at[k, 1], r_tok.at[k, 1], cycle(-k)),
            remote(meta_ref.at[k], ma.at[k], s_tok.at[k, 2], r_tok.at[k, 2], cycle(-k)),
        ]

    def xt_copies():
        return [
            remote(xt.at[:, 1 - c], xts, s_xt.at[0], r_xt.at[0], sib),
            remote(ct.at[:, 1 - c], cts, s_xt.at[1], r_xt.at[1], sib),
        ]

    def hid_copy(q, core):
        ref = hid.at[q, core]
        return remote(ref, ref, s_hid.at[q], r_hid.at[q], sib)

    def rs_right(q, t):
        return remote(part.at[q, t], rbr.at[q, t], s_rsr.at[q, t], r_rsr.at[q, t], right)

    def rs_left(q, t):
        return remote(part.at[q, t], rbl.at[q, t], s_rsl.at[q, t], r_rsl.at[q, t], left)

    def ret_copies(k, j):
        cut = (k, slice(None), pl.ds(j * td, td))
        return [
            remote(ob.at[cut], ro.at[cut], s_ret.at[k, j, 0], r_ret.at[k, j, 0], cycle(k)),
            remote(tb.at[cut], rt.at[cut], s_ret.at[k, j, 1], r_ret.at[k, j, 1], cycle(k)),
        ]

    def gate_copy(k):
        return remote(gb.at[k], rg.at[k], s_rg.at[k], r_rg.at[k], cycle(k))

    def ag_own(q):
        @pl.when(has_r)
        def _():
            ag_right(q, 0).start()

        @pl.when(has_l)
        def _():
            ag_left(q, 0).start()

        ag_sib(q, z, 0, c).start()

    def ag_step(q, i):
        @pl.when(z - 1 - i >= 0)
        def _():
            from_left(q, i).wait_recv()

            @pl.when(has_r)
            def _():
                ag_right(q, i + 1).start()

            ag_sib(q, z - 1 - i, 1 + i, c).start()

        @pl.when(z + 1 + i <= n - 1)
        def _():
            from_right(q, i).wait_recv()

            @pl.when(has_l)
            def _():
                ag_left(q, i + 1).start()

            ag_sib(q, z + 1 + i, n + i, c).start()

    def ag_join(q):
        ag_sib(q, z, 0, 1 - c).wait_recv()
        for i in range(n - 1):

            @pl.when(z - 1 - i >= 0)
            def _():
                ag_sib(q, z - 1 - i, 1 + i, 1 - c).wait_recv()

            @pl.when(z + 1 + i <= n - 1)
            def _():
                ag_sib(q, z + 1 + i, n + i, 1 - c).wait_recv()

    def rs_step(q, j):
        t = n - 1 - j

        @pl.when(t > z)
        def _():
            @pl.when(has_l)
            def _():
                rs_right(q, t).wait_recv()
                part[q, t] = (part[q, t].astype(F32) + rbr[q, t].astype(F32)).astype(BF16)

            rs_right(q, t).start()

        @pl.when(j < z)
        def _():
            @pl.when(has_r)
            def _():
                rs_left(q, j).wait_recv()
                part[q, j] = (part[q, j].astype(F32) + rbl[q, j].astype(F32)).astype(BF16)

            rs_left(q, j).start()

    def rs_finish(q):
        total = part[q, z].astype(F32)
        acc[...] = total

        @pl.when(has_l)
        def _():
            rs_right(q, z).wait_recv()
            acc[...] += rbr[q, z].astype(F32)

        @pl.when(has_r)
        def _():
            rs_left(q, z).wait_recv()
            acc[...] += rbl[q, z].astype(F32)

        done = acc[...].astype(BF16)
        gin_ref[:, q * qw : (q + 1) * qw] = done[:, 0:qw]
        gin_ref[:, ffw + q * qw : ffw + (q + 1) * qw] = done[:, qw : 2 * qw]
        gout_ref[:, q * qw : (q + 1) * qw] = done[:, 2 * qw : 3 * qw]

    def turn(k):
        cut = slice(k * rows, (k + 1) * rows)
        xt[:, :, :, cut] = xa[cut, :].T.reshape(n, 2, sr, rows)
        ct[:, :, :, cut] = ca[cut, :].T.reshape(n, 2, sr, rows)

    def pick_of(k):
        return jnp.where(
            lax.broadcasted_iota(jnp.int32, (rows, span), 0).astype(F32) == ma[k, 0:1, :], 1.0, 0.0
        )

    def forward(q, gates):
        pre = dot_nn(xa[...], w[q, :, 0 : 2 * qw])
        dc = dot_nn(ca[...], w[q, :, 2 * qw : 3 * qw])
        h, u = pre[:, :qw], pre[:, qw:]
        sig = jax.nn.sigmoid(h)
        act = h * sig
        a = act * u
        da = gates * dc
        hid[q, c, :, 0:qw] = (da * u * (sig * (1.0 + h * (1.0 - sig)))).astype(BF16)
        hid[q, c, :, qw : 2 * qw] = (da * act).astype(BF16)
        hid[q, c, :, 2 * qw : 3 * qw] = (gates * a).astype(BF16)
        hid_copy(q, c).start()
        return jnp.sum(a * dc, axis=1, keepdims=True)

    def terms(q):
        hid_copy(q, 1 - c).wait_recv()
        mine, theirs = hid[q, c], hid[q, 1 - c]

        def one(t, carry):
            part[q, t, :, 0 : 2 * qw] = (
                dot_nn(xt[t, c], mine[:, 0 : 2 * qw]) + dot_nn(xts[t], theirs[:, 0 : 2 * qw])
            ).astype(BF16)
            part[q, t, :, 2 * qw : 3 * qw] = (
                dot_nn(ct[t, c], mine[:, 2 * qw :]) + dot_nn(cts[t], theirs[:, 2 * qw :])
            ).astype(BF16)
            return carry

        lax.fori_loop(0, n, one, 0)

    for k in range(1, stops):
        for copy in tok_copies(k):
            copy.start()
    ag_own(0)
    xa[0:rows, :] = tok_ref[...]
    ca[0:rows, :] = cot_ref[...]
    ma[0] = meta_ref[0]
    turn(0)
    for i in range(n - 1):
        ag_step(0, i)
    if nq > 1:
        ag_own(1)
        for i in range(n - 1):
            ag_step(1, i)
    for k in range(1, stops):
        for copy in tok_copies(k):
            copy.wait_recv()
    if nq > 2:
        ag_own(2)
    for k in range(1, stops):
        turn(k)
    for copy in xt_copies():
        copy.start()
    gates = jnp.concatenate(
        [jnp.sum(pick_of(k) * ma[k, 1:2, :], axis=1, keepdims=True) for k in range(stops)]
    )
    gate_sum = jnp.zeros((stops * rows, 1), F32)
    for q in range(nq):
        if q >= 2:
            for i in range(n - 1):
                ag_step(q, i)
                rs_step(q - 2, i)
            if q + 1 < nq:
                ag_own(q + 1)
        ag_join(q)
        gate_sum = gate_sum + forward(q, gates)
        if q == 0:
            for copy in xt_copies():
                copy.wait_recv()
        if q < nq - 1:
            terms(q)

    for k in range(stops):
        gt = gate_sum[k * rows : (k + 1) * rows]
        row = jnp.sum(pick_of(k) * gt, axis=0, keepdims=True)
        if k == 0:
            gate_ref[0] = jnp.broadcast_to(row, (8, span))
        else:
            gb[k] = jnp.broadcast_to(row, (8, span))
            gate_copy(k).start()
    for j in range(tiles):
        cut = slice(j * td, (j + 1) * td)
        out = sum(dot_nt(hid[q, c, :, 2 * qw :], w[q, cut, 2 * qw :]) for q in range(nq))
        tok = sum(dot_nt(hid[q, c, :, : 2 * qw], w[q, cut, : 2 * qw]) for q in range(nq))
        o0[:, cut] = out[:rows]
        t0[:, cut] = tok[:rows]
        for k in range(1, stops):
            ob[k, :, cut] = out[k * rows : (k + 1) * rows].astype(BF16)
            tb[k, :, cut] = tok[k * rows : (k + 1) * rows].astype(BF16)
            for copy in ret_copies(k, j):
                copy.start()
    terms(nq - 1)
    for q in range(max(nq - 2, 0), nq):
        for i in range(n - 1):
            rs_step(q, i)

    for k in range(1, stops):
        gate_copy(k).wait_recv()
        gate_ref[k] = rg[k]
        for j in range(tiles):
            for copy in ret_copies(k, j):
                copy.wait_recv()
    mixed, tgrad = o0[...], t0[...]
    for k in range(1, stops):
        mixed = mixed + ro[k].astype(F32)
        tgrad = tgrad + rt[k].astype(F32)
    mixed_ref[...] = mixed.astype(BF16)
    tgrad_ref[...] = tgrad.astype(BF16)
    for q in range(nq):
        rs_finish(q)

    for k in range(1, stops):
        for copy in tok_copies(k):
            copy.wait_send()
        gate_copy(k).wait_send()
        for j in range(tiles):
            for copy in ret_copies(k, j):
                copy.wait_send()
    for copy in xt_copies():
        copy.wait_send()
    for q in range(nq):
        hid_copy(q, c).wait_send()
        ag_sib(q, z, 0, c).wait_send()
        for i in range(n - 1):

            @pl.when((z - i >= 0) & has_r)
            def _():
                ag_right(q, i).wait_send()

            @pl.when((z + i <= n - 1) & has_l)
            def _():
                ag_left(q, i).wait_send()

            @pl.when(z - 1 - i >= 0)
            def _():
                ag_sib(q, z - 1 - i, 1 + i, c).wait_send()

            @pl.when(z + 1 + i <= n - 1)
            def _():
                ag_sib(q, z + 1 + i, n + i, c).wait_send()

            @pl.when(n - 1 - i > z)
            def _():
                rs_right(q, n - 1 - i).wait_send()

            @pl.when(i < z)
            def _():
                rs_left(q, i).wait_send()


def body(n_exp, n_dp, tokens, cotangent, w_in, w_out, block_rows, block_gates, block_count):
    stops = block_count.shape[1]
    block = block_rows.shape[2]
    span = block_rows.shape[1] // stops * block
    rows, width = tokens.shape
    sr, ffw = w_out.shape[1:]
    n, nq, total = n_dp // 2, ffw // LANES, stops * rows
    tiles = width // next(t for t in (512, 256, 128) if width % t == 0)
    entries = block_rows.reshape(stops, span)
    gates = block_gates.reshape(stops, span)
    positions = jnp.arange(span, dtype=jnp.int32)
    live = positions[None, :] // block < block_count[0][:, None]
    ids = jnp.where(live, entries, -1).astype(F32)
    pick = jnp.arange(8)[None, :, None]
    meta = jnp.where(pick == 0, ids[:, None, :], gates[:, None, :])

    dma = pltpu.SemaphoreType.DMA
    vmem = pltpu.VMEM
    mixed, tgrad, gate, gin, gout = pl.pallas_call(
        functools.partial(kernel, (n_exp, n_dp, stops)),
        out_shape=(
            jax.ShapeDtypeStruct((rows, width), BF16),
            jax.ShapeDtypeStruct((rows, width), BF16),
            jax.ShapeDtypeStruct((stops, 8, span), F32),
            jax.ShapeDtypeStruct((sr, 2 * ffw), BF16),
            jax.ShapeDtypeStruct((sr, ffw), BF16),
        ),
        in_specs=[pl.BlockSpec(memory_space=vmem)] * 5,
        out_specs=(pl.BlockSpec(memory_space=vmem),) * 5,
        scratch_shapes=[
            vmem((total, width), BF16),
            vmem((total, width), BF16),
            vmem((stops, 8, span), F32),
            vmem((nq, n_dp * sr, 3 * LANES), BF16),
            vmem((n, 2, sr, total), BF16),
            vmem((n, 2, sr, total), BF16),
            vmem((n, sr, total), BF16),
            vmem((n, sr, total), BF16),
            vmem((nq, 2, total, 3 * LANES), BF16),
            vmem((nq, n, sr, 3 * LANES), BF16),
            vmem((nq, n, sr, 3 * LANES), BF16),
            vmem((nq, n, sr, 3 * LANES), BF16),
            vmem((rows, width), F32),
            vmem((rows, width), F32),
            vmem((stops, rows, width), BF16),
            vmem((stops, rows, width), BF16),
            vmem((stops, 8, span), F32),
            vmem((stops, rows, width), BF16),
            vmem((stops, rows, width), BF16),
            vmem((stops, 8, span), F32),
            vmem((sr, 3 * LANES), F32),
            dma((nq, n)),
            dma((nq, n)),
            dma((nq, n)),
            dma((nq, n)),
            dma((nq, 2 * n)),
            dma((nq, 2 * n)),
            dma((2,)),
            dma((2,)),
            dma((nq,)),
            dma((nq,)),
            dma((nq, n)),
            dma((nq, n)),
            dma((nq, n)),
            dma((nq, n)),
            dma((stops, 3)),
            dma((stops, 3)),
            dma((stops, tiles, 2)),
            dma((stops, tiles, 2)),
            dma((stops,)),
            dma((stops,)),
        ],
        compiler_params=pltpu.CompilerParams(
            collective_id=0, has_side_effects=True, vmem_limit_bytes=56 * 1024 * 1024
        ),
        cost_estimate=pl.CostEstimate(
            flops=6 * total * width * 3 * ffw, bytes_accessed=8 * rows * width, transcendentals=0
        ),
    )(tokens, cotangent, w_in[0], w_out[0], meta)
    return mixed, tgrad, gate[:, 0].reshape(block_rows.shape), gin[None], gout[None]


def solution(mesh):
    in_specs = (
        P(("expert", "dp"), None),
        P(("expert", "dp"), None),
        P("expert", "dp", None),
        P("expert", "dp", None),
        P(("expert", "dp"), None, None),
        P(("expert", "dp"), None, None),
        P(("expert", "dp"), None),
    )
    out_specs = (
        P(("expert", "dp"), None),
        P(("expert", "dp"), None),
        P(("expert", "dp"), None, None),
        P("expert", "dp", None),
        P("expert", "dp", None),
    )
    run = functools.partial(body, mesh.shape["expert"], mesh.shape["dp"])
    return jax.shard_map(run, mesh=mesh, in_specs=in_specs, out_specs=out_specs, check_vma=False)
```

time: 158 us -> 128 us (0.81)
  Pallas kernels: 0 us -> 118 us
  waiting for transfers between devices: 105 us -> 0 us
  between operations: 13.9 us -> 0.67 us
  starting transfers between devices: 10.6 us -> 0 us
  matrix products: 9.09 us -> 0 us
  other arithmetic: 8.28 us -> 0.75 us
  local copies, waits for them, and re-layouts: 10.7 us -> 8.24 us
    pallas_call x0 -> x1, Pallas kernels: none -> 118 us  [body(): pl.pallas_call(functools.partial(kernel, (n_exp, n_dp, stops)), out_shape...]
    ppermute x6 -> x0, waiting for transfers between devices: 41.4 us -> none  [shifted(): return lax.ppermute(block, axis, route)]
    all_gather x2 -> x0, waiting for transfers between devices: 37.9 us -> none  [the longest x1 22.7 us: body(): slab_out = lax.all_gather(w_out[0], 'dp', axis=0, tiled=True)]
    reduce_scatter x1 -> x0, waiting for transfers between devices: 24.5 us -> none  [body(): total = lax.psum_scatter(term, 'dp', scatter_dimension=0, tiled=True)]
    ppermute x6 -> x0, starting transfers between devices: 10.5 us -> none  [shifted(): return lax.ppermute(block, axis, route)]
    dot_general x6 -> x0, matrix products: 9.09 us -> none  [the longest x1 2.86 us: body(): dc = jnp.dot(c, slab_out, preferred_element_type=f32)]
    convert_element_type x2 -> x1, other arithmetic: 4.2 us -> 0.07 us  [body(): ids = jnp.where(live, entries, -1).astype(F32)]
    concatenate x2 -> x0, other arithmetic: 2.51 us -> none  [the longest x1 2.5 us: body(): jnp.concatenate([contract_rows(x, hg), contract_rows(c, ag)], axis=1)]
  transfers between devices with their start and end apart: 9 -> 0, of which waited for: 9 -> 0; matrix products, arithmetic and copies ran while one was open for 8% -> 0% of each run, Pallas kernels for 0% -> 0%
where the time goes in v2:
time: 128 us; the launch traced here: 127 us
  Pallas kernels  118 us (92%)
  local copies, waits for them, and re-layouts  8.24 us (6%)
    pallas_call x1, Pallas kernels, body(): pl.pallas_call(functools.partial(kernel, (n_exp, n_dp, stops)), out_shape...  118 us
    unnamed x16, local copies, waits for them, and re-layouts  6.7 us

profile of v2, /device:TPU:0, one launch (start us, length us, event | category | flops | bytes accessed | tf_op | source)
XLA Modules:
  0.0 127.5 jit_solution(1558690450201332013)
XLA Ops:
  0.6 0.0 copy-start.3
  0.7 0.7 copy-done.3
  1.3 0.0 copy-start.5
  1.3 0.1 reshape.88
  1.4 0.6 copy-done.5
  2.0 0.0 copy-start.4
  2.0 0.1 fusion
  2.0 0.6 copy-done.4
  2.7 0.1 broadcast_in_dim.42
  2.7 0.7 broadcast_select_fusion.meta_ref
  3.4 117.8 %shard_map.110 = (bf16[128,2048]{1,0:T(8,128)(2,1)}, bf16[128,2048]{1,0:T(8,128)(2,1)}, f32[2,8,128]{2,1,0:T(8,128)}, bf16[256,768]{1,0:T(8,128)(2,1)}, bf16[256,384]{1,0:T(8,128)(2,1)}) custom-call(bf16[128,2048]{1,0:T(8,128)(2,1)} %tok_ref.1, bf16[128,2048]{1,0:T(8,128)(2,1)} %cot_ref.1, bf16[256,768]{1,0:T(8,128)(2,1)} %bitcast.8, ...), custom_call_target="tpu_custom_call" | custom-call | flops 3623878656 | bytes 2097152 | tf_op jit(solution)/shard_map/pallas_call | solution.py:445
  121.2 0.7 slice_reduce_fusion
  121.9 0.7 reshape_squeeze.3
  122.6 0.0 copy-start
  122.6 1.9 %copy.16 = bf16[128,2048]{1,0:T(8,128)(2,1)} copy(bf16[128,2048]{1,0:T(8,128)(2,1)} %get-tuple-element.20) | data formatting | bytes 1048576
  124.5 0.0 copy-done
  124.5 0.0 copy-start.1
  124.5 0.8 copy.17
  125.3 0.4 copy-done.1
  125.7 0.0 copy-start.2
  125.7 0.7 copy.18
  126.5 0.3 copy-done.2
  126.8 0.7 copy.19
  (2 shorter events, 0.0 us)
Async XLA Ops:
  0.6 0.7 copy-start.3
  1.3 0.7 copy-start.5
  2.0 0.7 copy-start.4
  122.6 1.9 %copy-start = (bf16[128,2048]{1,0:T(8,128)(2,1)S(1)}, bf16[128,2048]{1,0:T(8,128)(2,1)}, u32[]{:S(2)}) copy-start(bf16[128,2048]{1,0:T(8,128)(2,1)} %get-tuple-element.21) | copy-start | bytes 1572868
  124.5 1.2 copy-start.1
  125.7 1.1 copy-start.2

commit v3 on v2

--- a/solution.py
+++ b/solution.py
@@ -316,13 +316,9 @@
         ag_step(0, i)
     if nq > 1:
         ag_own(1)
-        for i in range(n - 1):
-            ag_step(1, i)
     for k in range(1, stops):
         for copy in tok_copies(k):
             copy.wait_recv()
-    if nq > 2:
-        ag_own(2)
     for k in range(1, stops):
         turn(k)
     for copy in xt_copies():
@@ -332,19 +328,24 @@
     )
     gate_sum = jnp.zeros((stops * rows, 1), F32)
     for q in range(nq):
-        if q >= 2:
-            for i in range(n - 1):
+        if q >= 1:
+            if q > 1:
+                ag_step(q, 0)
+            rs_step(q - 1, 0)
+            for i in range(1, n - 1):
                 ag_step(q, i)
-                rs_step(q - 2, i)
+                rs_step(q - 1, i)
             if q + 1 < nq:
                 ag_own(q + 1)
         ag_join(q)
         gate_sum = gate_sum + forward(q, gates)
         if q == 0:
+            if nq > 1:
+                ag_step(1, 0)
             for copy in xt_copies():
                 copy.wait_recv()
-        if q < nq - 1:
-            terms(q)
+        terms(q)
+    rs_step(nq - 1, 0)
 
     for k in range(stops):
         gt = gate_sum[k * rows : (k + 1) * rows]
@@ -365,10 +366,8 @@
             tb[k, :, cut] = tok[k * rows : (k + 1) * rows].astype(BF16)
             for copy in ret_copies(k, j):
                 copy.start()
-    terms(nq - 1)
-    for q in range(max(nq - 2, 0), nq):
-        for i in range(n - 1):
-            rs_step(q, i)
+    for i in range(1, n - 1):
+        rs_step(nq - 1, i)
 
     for k in range(1, stops):
         gate_copy(k).wait_recv()

time: 128 us -> 147 us (1.15)
  the two profiles are of different devices: /device:TPU:0 before, /device:TPU:8 now
where the time goes in v3:
time: 147 us
  Pallas kernels  137 us (93%)
  local copies, waits for them, and re-layouts  8.24 us (6%)
    pallas_call x1, Pallas kernels, body(): pl.pallas_call(functools.partial(kernel, (n_exp, n_dp, stops)), out_shape...  137 us
    unnamed x16, local copies, waits for them, and re-layouts  6.7 us

profile of v3, /device:TPU:8, one launch (start us, length us, event | category | flops | bytes accessed | tf_op | source)
XLA Modules:
  0.0 146.8 jit_solution(6108049646868290083)
XLA Ops:
  0.6 0.0 copy-start.3
  0.7 0.7 copy-done.3
  1.3 0.0 copy-start.5
  1.3 0.1 reshape.88
  1.4 0.6 copy-done.5
  2.0 0.0 copy-start.4
  2.0 0.1 fusion
  2.0 0.6 copy-done.4
  2.7 0.1 broadcast_in_dim.42
  2.7 0.7 broadcast_select_fusion.meta_ref
  3.4 137.2 %shard_map.110 = (bf16[128,2048]{1,0:T(8,128)(2,1)}, bf16[128,2048]{1,0:T(8,128)(2,1)}, f32[2,8,128]{2,1,0:T(8,128)}, bf16[256,768]{1,0:T(8,128)(2,1)}, bf16[256,384]{1,0:T(8,128)(2,1)}) custom-call(bf16[128,2048]{1,0:T(8,128)(2,1)} %tok_ref.1, bf16[128,2048]{1,0:T(8,128)(2,1)} %cot_ref.1, bf16[256,768]{1,0:T(8,128)(2,1)} %bitcast.8, ...), custom_call_target="tpu_custom_call" | custom-call | flops 3623878656 | bytes 2097152 | tf_op jit(solution)/shard_map/pallas_call | solution.py:444
  140.6 0.7 slice_reduce_fusion
  141.3 0.7 reshape_squeeze.3
  141.9 0.0 copy-start
  141.9 1.9 %copy.16 = bf16[128,2048]{1,0:T(8,128)(2,1)} copy(bf16[128,2048]{1,0:T(8,128)(2,1)} %get-tuple-element.20) | data formatting | bytes 1048576
  143.9 0.0 copy-done
  143.9 0.0 copy-start.1
  143.9 0.8 copy.17
  144.7 0.4 copy-done.1
  145.1 0.0 copy-start.2
  145.1 0.7 copy.18
  145.8 0.3 copy-done.2
  146.1 0.7 copy.19
  (2 shorter events, 0.0 us)
Async XLA Ops:
  0.6 0.7 copy-start.3
  1.3 0.7 copy-start.5
  2.0 0.7 copy-start.4
  141.9 1.9 %copy-start = (bf16[128,2048]{1,0:T(8,128)(2,1)S(1)}, bf16[128,2048]{1,0:T(8,128)(2,1)}, u32[]{:S(2)}) copy-start(bf16[128,2048]{1,0:T(8,128)(2,1)} %get-tuple-element.21) | copy-start | bytes 1572868
  143.9 1.2 copy-start.1
  145.1 1.1 copy-start.2

commit v4 on v2

--- a/solution.py
+++ b/solution.py
@@ -53,10 +53,8 @@
     rt,
     rg,
     acc,
-    s_agr,
-    r_agr,
-    s_agl,
-    r_agl,
+    s_ag,
+    r_ag,
     s_sib,
     r_sib,
     s_xt,
@@ -97,6 +95,9 @@
     def cycle(k):
         return {"expert": (e + k) % n_exp, "dp": d}
 
+    def lane_peer(i):
+        return {"expert": e, "dp": 2 * ((z + i) % n) + c}
+
     def remote(src, dst, ss, rs, dev):
         return pltpu.make_async_remote_copy(
             src_ref=src, dst_ref=dst, send_sem=ss, recv_sem=rs, device_id=dev, device_id_type=MESH
@@ -108,44 +109,30 @@
     for k in offsets:
         pl.semaphore_signal(barrier, inc=1, device_id=cycle(k), device_id_type=MESH)
 
-    @pl.when(has_l)
-    def _():
-        pl.semaphore_signal(barrier, inc=1, device_id=left, device_id_type=MESH)
-
-    @pl.when(has_r)
-    def _():
-        pl.semaphore_signal(barrier, inc=1, device_id=right, device_id_type=MESH)
+    for i in range(1, n):
+        pl.semaphore_signal(barrier, inc=1, device_id=lane_peer(i), device_id_type=MESH)
 
     own = pl.ds(pl.multiple_of(d * sr, 16), sr)
     for q in range(nq):
         w[q, own, 0:qw] = win_ref[:, q * qw : (q + 1) * qw]
         w[q, own, qw : 2 * qw] = win_ref[:, ffw + q * qw : ffw + (q + 1) * qw]
         w[q, own, 2 * qw : 3 * qw] = wout_ref[:, q * qw : (q + 1) * qw]
-    neighbours = jnp.where(has_l, 1, 0) + jnp.where(has_r, 1, 0)
-    pl.semaphore_wait(barrier, 1 + len(offsets) + neighbours)
+    pl.semaphore_wait(barrier, n + len(offsets))
 
     def shard(q, chip, core):
         return w.at[q, pl.ds(pl.multiple_of((2 * chip + core) * sr, 16), sr)]
 
-    def ag_right(q, i):
-        ref = shard(q, z - i, c)
-        return remote(ref, ref, s_agr.at[q, i], r_agr.at[q, i], right)
-
-    def ag_left(q, i):
-        ref = shard(q, z + i, c)
-        return remote(ref, ref, s_agl.at[q, i], r_agl.at[q, i], left)
-
-    def from_left(q, i):
-        ref = shard(q, z - 1 - i, c)
-        return remote(ref, ref, s_agr.at[q, i], r_agr.at[q, i], left)
-
-    def from_right(q, i):
-        ref = shard(q, z + 1 + i, c)
-        return remote(ref, ref, s_agl.at[q, i], r_agl.at[q, i], right)
-
-    def ag_sib(q, chip, index, core):
-        ref = shard(q, chip, core)
-        return remote(ref, ref, s_sib.at[q, index], r_sib.at[q, index], sib)
+    def ag_send(q, i):
+        ref = shard(q, z, c)
+        return remote(ref, ref, s_ag.at[q, i], r_ag.at[q, i], lane_peer(i))
+
+    def ag_arrival(q, i):
+        ref = shard(q, (z + n - i) % n, c)
+        return remote(ref, ref, s_ag.at[q, i], r_ag.at[q, i], lane_peer(n - i))
+
+    def ag_sib(q, i, core):
+        ref = shard(q, (z + n - i) % n, core)
+        return remote(ref, ref, s_sib.at[q, i], r_sib.at[q, i], sib)
 
     def tok_copies(k):
         cut = pl.ds(k * rows, rows)
@@ -182,48 +169,16 @@
         return remote(gb.at[k], rg.at[k], s_rg.at[k], r_rg.at[k], cycle(k))
 
     def ag_own(q):
-        @pl.when(has_r)
-        def _():
-            ag_right(q, 0).start()
-
-        @pl.when(has_l)
-        def _():
-            ag_left(q, 0).start()
-
-        ag_sib(q, z, 0, c).start()
-
-    def ag_step(q, i):
-        @pl.when(z - 1 - i >= 0)
-        def _():
-            from_left(q, i).wait_recv()
-
-            @pl.when(has_r)
-            def _():
-                ag_right(q, i + 1).start()
-
-            ag_sib(q, z - 1 - i, 1 + i, c).start()
-
-        @pl.when(z + 1 + i <= n - 1)
-        def _():
-            from_right(q, i).wait_recv()
-
-            @pl.when(has_l)
-            def _():
-                ag_left(q, i + 1).start()
-
-            ag_sib(q, z + 1 + i, n + i, c).start()
+        for i in range(1, n):
+            ag_send(q, i).start()
+        ag_sib(q, 0, c).start()
 
     def ag_join(q):
-        ag_sib(q, z, 0, 1 - c).wait_recv()
-        for i in range(n - 1):
-
-            @pl.when(z - 1 - i >= 0)
-            def _():
-                ag_sib(q, z - 1 - i, 1 + i, 1 - c).wait_recv()
-
-            @pl.when(z + 1 + i <= n - 1)
-            def _():
-                ag_sib(q, z + 1 + i, n + i, 1 - c).wait_recv()
+        for i in range(1, n):
+            ag_arrival(q, i).wait_recv()
+            ag_sib(q, i, c).start()
+        for i in range(n):
+            ag_sib(q, i, 1 - c).wait_recv()
 
     def rs_step(q, j):
         t = n - 1 - j
@@ -312,17 +267,12 @@
     ca[0:rows, :] = cot_ref[...]
     ma[0] = meta_ref[0]
     turn(0)
-    for i in range(n - 1):
-        ag_step(0, i)
+    ag_join(0)
     if nq > 1:
         ag_own(1)
-        for i in range(n - 1):
-            ag_step(1, i)
     for k in range(1, stops):
         for copy in tok_copies(k):
             copy.wait_recv()
-    if nq > 2:
-        ag_own(2)
     for k in range(1, stops):
         turn(k)
     for copy in xt_copies():
@@ -332,19 +282,20 @@
     )
     gate_sum = jnp.zeros((stops * rows, 1), F32)
     for q in range(nq):
-        if q >= 2:
-            for i in range(n - 1):
-                ag_step(q, i)
-                rs_step(q - 2, i)
-            if q + 1 < nq:
-                ag_own(q + 1)
-        ag_join(q)
+        if q > 0:
+            ag_join(q)
         gate_sum = gate_sum + forward(q, gates)
         if q == 0:
             for copy in xt_copies():
                 copy.wait_recv()
         if q < nq - 1:
             terms(q)
+            rs_step(q, 0)
+            if q + 2 < nq:
+                ag_own(q + 2)
+            if q < nq - 2:
+                for i in range(1, n - 1):
+                    rs_step(q, i)
 
     for k in range(stops):
         gt = gate_sum[k * rows : (k + 1) * rows]
@@ -367,7 +318,7 @@
                 copy.start()
     terms(nq - 1)
     for q in range(max(nq - 2, 0), nq):
-        for i in range(n - 1):
+        for i in range(0 if q == nq - 1 else 1, n - 1):
             rs_step(q, i)
 
     for k in range(1, stops):
@@ -396,24 +347,11 @@
         copy.wait_send()
     for q in range(nq):
         hid_copy(q, c).wait_send()
-        ag_sib(q, z, 0, c).wait_send()
+        for i in range(n):
+            ag_sib(q, i, c).wait_send()
+        for i in range(1, n):
+            ag_send(q, i).wait_send()
         for i in range(n - 1):
-
-            @pl.when((z - i >= 0) & has_r)
-            def _():
-                ag_right(q, i).wait_send()
-
-            @pl.when((z + i <= n - 1) & has_l)
-            def _():
-                ag_left(q, i).wait_send()
-
-            @pl.when(z - 1 - i >= 0)
-            def _():
-                ag_sib(q, z - 1 - i, 1 + i, c).wait_send()
-
-            @pl.when(z + 1 + i <= n - 1)
-            def _():
-                ag_sib(q, z + 1 + i, n + i, c).wait_send()
 
             @pl.when(n - 1 - i > z)
             def _():
@@ -479,8 +417,6 @@
             dma((nq, n)),
             dma((nq, n)),
             dma((nq, n)),
-            dma((nq, 2 * n)),
-            dma((nq, 2 * n)),
             dma((2,)),
             dma((2,)),
             dma((nq,)),

time: 128 us -> 129 us (level)
    pallas_call x1, Pallas kernels: 118 us -> 119 us  [body(): pl.pallas_call(functools.partial(kernel, (n_exp, n_dp, stops)), out_shape...]
where the time goes in v4:
time: 129 us
  Pallas kernels  119 us (92%)
  local copies, waits for them, and re-layouts  8.24 us (6%)
    pallas_call x1, Pallas kernels, body(): pl.pallas_call(functools.partial(kernel, (n_exp, n_dp, stops)), out_shape...  119 us
    unnamed x16, local copies, waits for them, and re-layouts  6.7 us

profile of v4, /device:TPU:0, one launch (start us, length us, event | category | flops | bytes accessed | tf_op | source)
XLA Modules:
  0.0 128.9 jit_solution(16892080042413231342)
XLA Ops:
  0.6 0.0 copy-start.3
  0.7 0.7 copy-done.3
  1.3 0.0 copy-start.5
  1.3 0.1 reshape.88
  1.4 0.6 copy-done.5
  2.0 0.0 copy-start.4
  2.0 0.1 fusion
  2.0 0.6 copy-done.4
  2.7 0.1 broadcast_in_dim.42
  2.7 0.7 broadcast_select_fusion.meta_ref
  3.4 119.3 %shard_map.110 = (bf16[128,2048]{1,0:T(8,128)(2,1)}, bf16[128,2048]{1,0:T(8,128)(2,1)}, f32[2,8,128]{2,1,0:T(8,128)}, bf16[256,768]{1,0:T(8,128)(2,1)}, bf16[256,384]{1,0:T(8,128)(2,1)}) custom-call(bf16[128,2048]{1,0:T(8,128)(2,1)} %tok_ref.1, bf16[128,2048]{1,0:T(8,128)(2,1)} %cot_ref.1, bf16[256,768]{1,0:T(8,128)(2,1)} %bitcast.8, ...), custom_call_target="tpu_custom_call" | custom-call | flops 3623878656 | bytes 2097152 | tf_op jit(solution)/shard_map/pallas_call | solution.py:383
  122.7 0.7 slice_reduce_fusion
  123.4 0.7 reshape_squeeze.3
  124.1 0.0 copy-start
  124.1 1.9 %copy.16 = bf16[128,2048]{1,0:T(8,128)(2,1)} copy(bf16[128,2048]{1,0:T(8,128)(2,1)} %get-tuple-element.20) | data formatting | bytes 1048576
  126.0 0.0 copy-done
  126.0 0.0 copy-start.1
  126.0 0.8 copy.17
  126.8 0.4 copy-done.1
  127.2 0.0 copy-start.2
  127.2 0.7 copy.18
  127.9 0.3 copy-done.2
  128.3 0.7 copy.19
  (2 shorter events, 0.0 us)
Async XLA Ops:
  0.6 0.7 copy-start.3
  1.3 0.7 copy-start.5
  2.0 0.7 copy-start.4
  124.1 1.9 %copy-start = (bf16[128,2048]{1,0:T(8,128)(2,1)S(1)}, bf16[128,2048]{1,0:T(8,128)(2,1)}, u32[]{:S(2)}) copy-start(bf16[128,2048]{1,0:T(8,128)(2,1)} %get-tuple-element.21) | copy-start | bytes 1572868
  126.0 1.2 copy-start.1
  127.2 1.1 copy-start.2

commit v5 on v4

--- a/solution.py
+++ b/solution.py
@@ -180,11 +180,11 @@
         for i in range(n):
             ag_sib(q, i, 1 - c).wait_recv()
 
-    def rs_step(q, j):
-        t = n - 1 - j
-
-        @pl.when(t > z)
+    def rs_step(q, i):
+        @pl.when(i >= z)
         def _():
+            t = n - 1 - i + z
+
             @pl.when(has_l)
             def _():
                 rs_right(q, t).wait_recv()
@@ -192,14 +192,16 @@
 
             rs_right(q, t).start()
 
-        @pl.when(j < z)
+        @pl.when(i >= n - 1 - z)
         def _():
+            t = i - (n - 1 - z)
+
             @pl.when(has_r)
             def _():
-                rs_left(q, j).wait_recv()
-                part[q, j] = (part[q, j].astype(F32) + rbl[q, j].astype(F32)).astype(BF16)
-
-            rs_left(q, j).start()
+                rs_left(q, t).wait_recv()
+                part[q, t] = (part[q, t].astype(F32) + rbl[q, t].astype(F32)).astype(BF16)
+
+            rs_left(q, t).start()
 
     def rs_finish(q):
         total = part[q, z].astype(F32)
@@ -317,9 +319,11 @@
             for copy in ret_copies(k, j):
                 copy.start()
     terms(nq - 1)
-    for q in range(max(nq - 2, 0), nq):
-        for i in range(0 if q == nq - 1 else 1, n - 1):
-            rs_step(q, i)
+    rs_step(nq - 1, 0)
+    for i in range(1, n - 1):
+        if nq > 1:
+            rs_step(nq - 2, i)
+        rs_step(nq - 1, i)
 
     for k in range(1, stops):
         gate_copy(k).wait_recv()

time: 129 us -> 110 us (0.85)
  the two profiles are of different devices: /device:TPU:0 before, /device:TPU:16 now
where the time goes in v5:
time: 110 us; the launch traced here: 109 us
  Pallas kernels  99.6 us (91%)
  local copies, waits for them, and re-layouts  8.24 us (7%)
    pallas_call x1, Pallas kernels, body(): pl.pallas_call(functools.partial(kernel, (n_exp, n_dp, stops)), out_shape...  99.6 us
    unnamed x16, local copies, waits for them, and re-layouts  6.7 us

profile of v5, /device:TPU:16, one launch (start us, length us, event | category | flops | bytes accessed | tf_op | source)
XLA Modules:
  0.0 109.2 jit_solution(10801728672764000671)
XLA Ops:
  0.6 0.0 copy-start.3
  0.7 0.7 copy-done.3
  1.3 0.0 copy-start.5
  1.3 0.1 reshape.88
  1.4 0.6 copy-done.5
  2.0 0.0 copy-start.4
  2.0 0.1 fusion
  2.0 0.6 copy-done.4
  2.7 0.1 broadcast_in_dim.42
  2.7 0.7 broadcast_select_fusion.meta_ref
  3.4 99.6 %shard_map.110 = (bf16[128,2048]{1,0:T(8,128)(2,1)}, bf16[128,2048]{1,0:T(8,128)(2,1)}, f32[2,8,128]{2,1,0:T(8,128)}, bf16[256,768]{1,0:T(8,128)(2,1)}, bf16[256,384]{1,0:T(8,128)(2,1)}) custom-call(bf16[128,2048]{1,0:T(8,128)(2,1)} %tok_ref.1, bf16[128,2048]{1,0:T(8,128)(2,1)} %cot_ref.1, bf16[256,768]{1,0:T(8,128)(2,1)} %bitcast.8, ...), custom_call_target="tpu_custom_call" | custom-call | flops 3623878656 | bytes 2097152 | tf_op jit(solution)/shard_map/pallas_call | solution.py:387
  103.0 0.7 slice_reduce_fusion
  103.7 0.7 reshape_squeeze.3
  104.4 0.0 copy-start
  104.4 1.9 %copy.16 = bf16[128,2048]{1,0:T(8,128)(2,1)} copy(bf16[128,2048]{1,0:T(8,128)(2,1)} %get-tuple-element.20) | data formatting | bytes 1048576
  106.3 0.0 copy-done
  106.3 0.0 copy-start.1
  106.3 0.8 copy.17
  107.1 0.4 copy-done.1
  107.5 0.0 copy-start.2
  107.5 0.7 copy.18
  108.2 0.3 copy-done.2
  108.6 0.7 copy.19
  (2 shorter events, 0.0 us)
Async XLA Ops:
  0.6 0.7 copy-start.3
  1.3 0.7 copy-start.5
  2.0 0.7 copy-start.4
  104.4 1.9 %copy-start = (bf16[128,2048]{1,0:T(8,128)(2,1)S(1)}, bf16[128,2048]{1,0:T(8,128)(2,1)}, u32[]{:S(2)}) copy-start(bf16[128,2048]{1,0:T(8,128)(2,1)} %get-tuple-element.21) | copy-start | bytes 1572868
  106.3 1.2 %copy-start.1 = (bf16[256,768]{1,0:T(8,128)(2,1)S(1)}, bf16[256,768]{1,0:T(8,128)(2,1)}, u32[]{:S(2)}) copy-start(bf16[256,768]{1,0:T(8,128)(2,1)} %get-tuple-element.13) | copy-start | bytes 1179652
  107.5 1.1 copy-start.2
